TPU v7x, 256 devices: a whole 4x4x8 slice. The times are simulated.
256 devices in a mesh: row: 32 (over z, y), col: 8 (over x, core).
Axes of the slice: x: 4, y: 4, z: 8, core: 2. Of those that a mesh axis runs over, the one named last changes fastest.
Arguments:
- top_inverse: float32 [8192, 8192], P('row', 'col'), as said below
- panels: float32 [8192, 8192], P('row', 'col'), may hold values from -0.24 to 0.24
- fill_pattern: int32 [64, 64], P('col'), may hold values from 0 to 1, as said below
- diagonal_part: float32 [8192, 128], P('col'), as said below
Outputs:
- offdiag_inverse: float32 [8192, 8192], P('row', 'col')
- diagonal_inverse: float32 [8192, 128], P('col')
Inputs may be any that keep to these rules, and one draw needn't show every extreme that they name: top_inverse is exactly symmetric. `fill_pattern`: every second-level supernode couples to at least one top block. Each 128 x 128 block of diagonal_part is exactly symmetric.
All inputs are finite; a program needn't handle non-finite values.
Results may differ from a plain program's by a relative error of at most 0.000075.
Values sent between devices are 32-bit elements; how exact they have to be, the bound alone decides.
A program may use at most 128 MiB of HBM per device.

v0:
```python
import jax
import jax.numpy as jnp
from jax import lax
from jax.sharding import PartitionSpec as P

BLOCK = 128


def local(top_inverse, panels, fill_pattern, diagonal_part):
    rows_here = top_inverse.shape[0]
    cols_here = panels.shape[1]
    child_count = cols_here // BLOCK
    row_count = rows_here // BLOCK
    first_block = lax.axis_index("row") * row_count
    local_fill = lax.dynamic_slice_in_dim(fill_pattern, first_block, row_count, 1)
    block_mask = jnp.broadcast_to(
        local_fill.T.astype(jnp.float32)[:, None, :, None], (row_count, BLOCK, child_count, BLOCK)
    ).reshape(rows_here, cols_here)
    scaled_panel = panels * block_mask
    block_row = lax.all_gather(top_inverse, "col", axis=1, tiled=True)
    product = jnp.dot(
        block_row,
        lax.all_gather(scaled_panel, "row", axis=0, tiled=True),
        precision=lax.Precision.HIGHEST,
        preferred_element_type=jnp.float32,
    )
    offdiag_inverse = -product * block_mask
    diag_terms = jnp.einsum(
        "mkb,mkc->kbc",
        scaled_panel.reshape(rows_here, child_count, BLOCK),
        offdiag_inverse.reshape(rows_here, child_count, BLOCK),
        precision=lax.Precision.HIGHEST,
    ).reshape(child_count * BLOCK, BLOCK)
    summed = lax.psum(diag_terms, "row")
    diagonal_inverse = diagonal_part - summed
    return (offdiag_inverse, diagonal_inverse)


def solution(mesh):
    in_specs = (P("row", "col"), P("row", "col"), P("col", None), P("col", None))
    out_specs = (P("row", "col"), P("col", None))
    return jax.shard_map(local, mesh=mesh, in_specs=in_specs, out_specs=out_specs, check_vma=False)
```

profile of v0, /device:TPU:2, one launch (start us, length us, event | category | flops | bytes accessed | tf_op | source)
XLA Modules:
  0.0 499.6 jit_solution(141219759727936969)
XLA Ops:
  7.2 0.0 all-gather.5.cloned.1.call-start
  7.2 0.7 all-gather.5.cloned.1.call-update
  7.9 0.0 all-gather.3.cloned.1.call-start
  7.9 1.6 copy.6
  9.5 0.8 convert_bitcast_fusion
  10.3 0.3 broadcast_in_dim.2
  10.6 1.1 bitcast_multiply_fusion
  11.7 0.0 copy-start
  11.7 0.0 all-gather.3.cloned.1.call-update
  11.8 0.0 all-reduce.2.cloned.1.call-start
  11.8 52.5 %all-gather.5.cloned.1.call-done = f32[256,8192]{1,0:T(8,128)} async-done(((f32[256,1024]{1,0:T(8,128)}), f32[256,8192]{1,0:T(8,128)}) %all-gather.5.cloned.1.call-update) | async-done | bytes 8388624 | tf_op jit(solution)/shard_map/all_gather | solution.py:20
  64.3 249.5 %all-gather.3.cloned.1.call-done = f32[8192,1024]{0,1:T(8,128)} async-done(((f32[256,1024]{0,1:T(8,128)}), f32[8192,1024]{0,1:T(8,128)}) %all-gather.3.cloned.1.call-update) | async-done | bytes 33554448 | tf_op jit(solution)/shard_map/all_gather | solution.py:23
  313.8 30.9 %fusion.1 = f32[256,1024]{0,1:T(8,128)S(1)} fusion(f32[8192,1024]{0,1:T(8,128)} %all-gather.3.cloned.1.call-done, f32[256,8192]{1,0:T(8,128)} %all-gather.5.cloned.1.call-done, f32[128,8,2,128]{3,2,1,0:T(2,128)S(1)} %bitcast.21), kind=kOutput, calls=%fused_computation.2 | convolution fusion | flops 25770328064 | bytes 44040192 | tf_op jit(solution)/shard_map/dot_general | solution.py:21
  344.7 0.0 copy-done
  344.7 1.9 fusion.2
  346.6 0.0 all-reduce.2.cloned.1.call-update
  346.6 1.3 copy.8
  347.9 143.1 %all-reduce.2.cloned.1.call-done = f32[1024,128]{1,0:T(8,128)} async-done(((f32[1024,128]{1,0:T(8,128)}), f32[1024,128]{1,0:T(8,128)}) %all-reduce.2.cloned.1.call-update) | async-done | bytes 524304 | tf_op jit(solution)/shard_map/psum | solution.py:34
  491.1 2.0 sub.3
Async XLA Ops:
  7.2 57.1 %all-gather.5.cloned.1.call-start = ((), (), s32[]{:S(2)}) async-start(), calls=%async_computation.1 | async-start | bytes 9437184 | tf_op jit(solution)/shard_map/all_gather | solution.py:20
  7.9 305.9 %all-gather.3.cloned.1.call-start = ((), (), s32[]{:S(2)}) async-start(), calls=%async_computation | async-start | bytes 34603008 | tf_op jit(solution)/shard_map/all_gather | solution.py:23
  11.7 332.9 %copy-start = (f32[256,1024]{0,1:T(8,128)S(1)}, f32[256,1024]{0,1:T(8,128)}, u32[]{:S(2)}) copy-start(f32[256,1024]{0,1:T(8,128)} %bitcast_multiply_fusion) | copy-start | bytes 3145732
  11.8 479.3 %all-reduce.2.cloned.1.call-start = ((), (), s32[]{:S(2)}) async-start(), calls=%async_computation.2 | async-start | bytes 1048576 | tf_op jit(solution)/shard_map/psum | solution.py:34
Sparse Core Ops, SparseCore 0:
  9.8 54.4 all-gather.4
  67.3 246.3 all-gather.2
  346.7 144.2 all-reduce.1
where the time goes:
time: 500 us
  waiting for transfers between devices  446 us (89%)
  matrix products  32.8 us (7%)
  between operations  13.8 us (3%)
    all_gather x1, waiting for transfers between devices, local(): lax.all_gather(scaled_panel, 'row', axis=0, tiled=True)  249 us
    psum x1, waiting for transfers between devices, local(): summed = lax.psum(diag_terms, 'row')  143 us
    all_gather x1, waiting for transfers between devices, local(): block_row = lax.all_gather(top_inverse, 'col', axis=1, tiled=True)  52.5 us
    dot_general x1, matrix products, local(): jnp.dot(block_row, lax.all_gather(scaled_panel, 'row', axis=0, tiled=True...  30.9 us
  transfers between devices with their start and end apart: 3, of which 3 were waited for; matrix products, arithmetic and copies ran while one was open for 1% of the time, Pallas kernels for 0%

commit v1 on v0

v1 whole, which is shorter than its diff:
```python
import functools

import jax
import jax.numpy as jnp
from jax import lax
from jax.experimental import pallas as pl
from jax.experimental.pallas import tpu as pltpu
from jax.sharding import PartitionSpec as P

BLOCK = 128
Z, Y, X, CORES = 8, 4, 4, 2
ROWS = 2 * BLOCK
CHUNKS = 8
WAVES = ((0, 1), (2, 3), (4, 5), (6, 7))
GROUPS = 4
LINK = 90e3
HOP = 1.5


def steps(way, q):
    return 4 if q % 2 == way else 3


def zslot(way, s):
    return s if way == 0 else (Z - s) % Z


def arrival_of(q, d):
    if d < 4 or (d == 4 and q % 2 == 0):
        return ("z", 0, q, d - 1)
    return ("z", 1, q, Z - 1 - d)


class Plan:
    def __init__(self):
        self.tasks = []

    def add(self, name, rank, after=(), needs=(), sends=(), cost=0.0, gate=None):
        self.tasks.append(
            dict(name=name, rank=rank, after=after, needs=needs, sends=sends, cost=cost, gate=gate)
        )

    def order(self):
        now, free, arrived, done, result = 0.0, {}, {}, set(), []
        left = list(self.tasks)
        while left:
            best = None
            for task in left:
                if not all(n in done for n in task["after"]) or not all(n in arrived for n in task["needs"]):
                    continue
                ready = max([arrived[n] for n in task["needs"]], default=0.0)
                if task["gate"] is not None:
                    link, depth = task["gate"]
                    ready = max(ready, free.get(link, 0.0) - depth)
                ready = max(ready, now)
                key = (ready, task["rank"])
                if best is None or key < best[0]:
                    best = (key, task)
            (ready, _), task = best
            now = ready + task["cost"]
            for ident, link, size in task["sends"]:
                now += 0.05
                if link is None:
                    arrived[ident] = now + 2.5
                else:
                    rate = 6 * LINK if link == "s" else LINK
                    begin = max(now, free.get(link, 0.0))
                    free[link] = begin + size / rate
                    arrived[ident] = free[link] + HOP
            done.add(task["name"])
            left.remove(task)
            result.append((ready, task))
        return result, now


def make_plan():
    plan = Plan()
    piece = ROWS * BLOCK * 4 * CORES
    for q in range(CHUNKS):
        plan.add(("mask", q), (1, q) if q else (0, 0), cost=0.15)
        for way in range(2):
            plan.add(
                ("zown", way, q), (0, 1, way) if q == 0 else (2, q, way),
                after=[("mask", q)] + ([("zown", way, q - 1)] if q else []),
                sends=[(("z", way, q, 0), ("z", way), piece)], gate=(("z", way), 5.5),
            )
            for s in range(1, steps(way, q)):
                plan.add(
                    ("zfwd", way, q, s), (1, q, s), needs=[("z", way, q, s - 1)],
                    sends=[(("z", way, q, s), ("z", way), piece)],
                )
    block = ROWS * ROWS * 4 * CORES
    plan.add(
        ("a2a",), (0, 2),
        sends=[(("a", 3), ("y", 0), block), (("a", 1), ("y", 1), block), (("a", 2), ("y", 0), 2 * block)],
    )
    plan.add(("acopy",), (0, 3), cost=0.15)
    for j in range(Y):
        plan.add(
            ("xown", j), (0, 4), after=[("acopy",)], needs=[("a", j)] if j else [],
            sends=[(("x", 1, j), ("x", 0), block), (("x", 3, j), ("x", 1), block), (("s", 0, j), "s", block // 2)],
        )
        for e in (1, 3):
            sends = [(("s", e, j), "s", block // 2)]
            if (e == 1) == (j in (0, 3)):
                sends.append((("x", 2, j), ("x", e // 2), block))
            plan.add(("xfwd", e, j), (0, 5), needs=[("x", e, j)], sends=sends)
        plan.add(("xfwd", 2, j), (0, 5), needs=[("x", 2, j)], sends=[(("s", 2, j), "s", block // 2)])
    for e in range(X):
        for k in range(CORES):
            needs = [("s", e, j) if k else ("x", e, j) for j in range(Y)]
            if (e, k) == (0, 0):
                needs = [("a", j) for j in range(1, Y)]
            plan.add(("aconv", e, k), (3,), after=[("acopy",)], needs=needs, cost=0.5)
    for w, wave in enumerate(WAVES):
        width = len(wave) * BLOCK
        for d in range(Z):
            needs = [arrival_of(q, d) for q in wave] if d else []
            after = [("mask", q) for q in wave]
            after += [("mm", w - 2, j) for j in range(Y)] if w >= 2 else []
            plan.add(("pconv", w, d), (4, w), after=after, needs=needs, cost=0.15)
        half = ROWS // 2 * width * 4 * CORES
        after = [("pconv", w, d) for d in range(Z)] + [("aconv", e, k) for e in range(X) for k in range(CORES)]
        for j, sends in (
            (2, [(("r1", w, 0), ("y", 0), half), (("r1", w, 1), ("y", 1), half)]),
            (1, [(("r2", w, 0, 1), ("y", 0), half)]),
            (3, [(("r2", w, 1, 0), ("y", 1), half)]),
            (0, []),
        ):
            plan.add(("mm", w, j), (5, w, (2, 1, 3, 0).index(j)), after=after, sends=sends, cost=1.1)
        for way in range(2):
            plan.add(
                ("radd", w, way), (2, 0), after=[("mm", w, 1 + 2 * way)], needs=[("r1", w, way)],
                sends=[(("r2", w, way, way), ("y", way), half)], cost=0.1,
            )
        plan.add(
            ("fin", w), (2, 1), after=[("mm", w, 0), ("radd", w, 0), ("radd", w, 1)],
            needs=[("r2", w, way, h) for way in range(2) for h in range(2)], cost=0.8,
        )
    for g in range(GROUPS):
        owners = [("fin", w) for w, wave in enumerate(WAVES) if set(wave) & {2 * g, 2 * g + 1}]
        plan.add(("d1", g), (2, 2), after=owners, sends=[(("d1", g, j), None, 0) for j in (1, 3, 2)])
        plan.add(
            ("d2", g), (2, 2), needs=[("d1", g, j) for j in range(1, Y)],
            sends=[(("d2", g, i), None, 0) for i in range(1, Z)], cost=0.1,
        )
        plan.add(
            ("d3", g), (2, 2), needs=[("d2", g, i) for i in range(1, Z)],
            sends=[(("d3", g, i), None, 0) for i in range(1, Z)], cost=0.1,
        )
        plan.add(
            ("d4", g), (2, 2), needs=[("d3", g, i) for i in range(1, Z)],
            sends=[(("d4", g, j), None, 0) for j in range(1, Y)],
        )
        plan.add(("d5", g), (2, 2), needs=[("d4", g, j) for j in range(1, Y)], cost=0.1)
    return plan


def split(v):
    high = v.astype(jnp.bfloat16)
    return high, (v - high.astype(jnp.float32)).astype(jnp.bfloat16)


def dot(a, b):
    return jnp.dot(a, b, preferred_element_type=jnp.float32)


def kernel(order, a_ref, p_ref, fill_ref, d_ref, x_ref, g_ref, *scratch):
    (agat, ahi, alo, pgat, phi, plo, t, dr1, s1, dr2, res, send_sem, recv_sem), waves = scratch[:13], scratch[13:]
    xp, xr1, xr2 = waves[0::3], waves[1::3], waves[2::3]
    r, c = lax.axis_index("row"), lax.axis_index("col")
    z, y, x, core = lax.div(r, Y), lax.rem(r, Y), lax.div(c, CORES), lax.rem(c, CORES)

    def device(dz=0, dy=0, dx=0, dc=0):
        return {
            "row": lax.rem(z + dz, Z) * Y + lax.rem(y + dy, Y),
            "col": lax.rem(x + dx, X) * CORES + lax.rem(core + dc, CORES),
        }

    def part(index, size):
        return pl.ds(pl.multiple_of(index * size, size), size)

    partners = [device(dz=i) for i in range(1, Z)] + [device(dy=j) for j in range(1, Y)]
    partners += [device(dx=1), device(dx=X - 1), device(dc=1)]
    barrier = pltpu.get_barrier_semaphore()
    for partner in partners:
        pl.semaphore_signal(barrier, inc=1, device_id=partner, device_id_type=pl.DeviceIdType.MESH)
    pl.semaphore_wait(barrier, len(partners))

    half, quarter, eighth = ROWS // 2, 2 * BLOCK // Y, 2 * BLOCK // Y // Z

    def ends(ident):
        kind, *at = ident
        if kind == "z":
            way, q, s = at
            return (
                pgat.at[q, zslot(way, s)], pgat.at[q, zslot(way, s + 1)],
                device(dz=1 if way == 0 else Z - 1),
            )
        if kind == "a":
            (j,) = at
            i = Y - j
            return a_ref.at[:, part(lax.rem(y + i, Y), ROWS)], agat.at[0, 0, j], device(dy=i)
        if kind == "x":
            e, j = at
            if e == 2:
                way = 0 if j in (0, 3) else 1
                source = agat.at[1 + 2 * way, 0, j]
            else:
                way, source = e // 2, agat.at[0, 0, j]
            return source, agat.at[e, 0, j], device(dx=1 if way == 0 else X - 1)
        if kind == "s":
            e, j = at
            return agat.at[e, 0, j], agat.at[e, 1, j], device(dc=1)
        if kind == "r1":
            w, way = at
            return xp[w].at[2, pl.ds(way * half, half)], xr1[w].at[way], device(dy=1 if way == 0 else Y - 1)
        if kind == "r2":
            w, way, h = at
            rows = pl.ds(h * half, half)
            return xp[w].at[1 + 2 * way, rows], xr2[w].at[way, rows], device(dy=1 if way == 0 else Y - 1)
        if kind == "d1":
            g, j = at
            return t.at[g, part(lax.rem(y + j, Y), quarter)], dr1.at[g, j - 1], device(dy=j)
        if kind == "d2":
            g, i = at
            return s1.at[g, part(lax.rem(z + i, Z), eighth)], dr2.at[g, i - 1], device(dz=i)
        if kind == "d3":
            g, i = at
            where = res.at[g, y, part(z, eighth)]
            return where, where, device(dz=i)
        g, j = at
        return res.at[g, y], res.at[g, y], device(dy=j)

    def fill(q, i):
        return fill_ref[q, 2 * r + i].astype(jnp.float32)

    def body(name):
        kind, *at = name
        if kind == "mask":
            (q,) = at
            for i in range(2):
                rows = slice(i * BLOCK, (i + 1) * BLOCK)
                pgat[q, 0, rows] = p_ref[rows, q * BLOCK : (q + 1) * BLOCK] * fill(q, i)
        elif kind == "acopy":
            agat[0, 0, 0] = a_ref[:, part(y, ROWS)]
        elif kind == "aconv":
            e, k = at
            owner = lax.rem(x + X - e, X) * CORES + lax.rem(core + k, CORES)
            place = part(lax.rem(z + Z - owner, Z), ROWS)

            @pl.loop(0, Y)
            def _(j):
                high, low = split(agat[e, k, j])
                ahi[part(j, ROWS), place] = high
                alo[part(j, ROWS), place] = low

        elif kind == "pconv":
            w, d = at
            for i, q in enumerate(WAVES[w]):
                high, low = split(pgat[q, d])
                phi[w % 2, d * ROWS : (d + 1) * ROWS, i * BLOCK : (i + 1) * BLOCK] = high
                plo[w % 2, d * ROWS : (d + 1) * ROWS, i * BLOCK : (i + 1) * BLOCK] = low
        elif kind == "mm":
            w, j = at
            cols = slice(0, len(WAVES[w]) * BLOCK)
            rows = slice(j * ROWS, (j + 1) * ROWS)
            high, low = phi[w % 2, :, cols], plo[w % 2, :, cols]
            xp[w][j] = dot(ahi[rows], high) + dot(ahi[rows], low) + dot(alo[rows], high)
        elif kind == "radd":
            w, way = at
            rows = slice(way * half, (way + 1) * half)
            xp[w][1 + 2 * way, rows] += xr1[w][way]
        elif kind == "fin":
            (w,) = at
            total = xp[w][0] + xr2[w][0] + xr2[w][1]
            for n, q in enumerate(WAVES[w]):
                mine = total[:, n * BLOCK : (n + 1) * BLOCK]
                mine = jnp.concatenate([mine[i * BLOCK : (i + 1) * BLOCK] * -fill(q, i) for i in range(2)], axis=0)
                x_ref[:, q * BLOCK : (q + 1) * BLOCK] = mine
                t[q // 2, q % 2 * BLOCK : (q % 2 + 1) * BLOCK] = lax.dot_general(
                    pgat[q, 0], mine, (((0,), (0,)), ((), ())),
                    precision=lax.Precision.HIGHEST, preferred_element_type=jnp.float32,
                )
        elif kind == "d2":
            (g,) = at
            s1[g] = t[g, part(y, quarter)] + dr1[g, 0] + dr1[g, 1] + dr1[g, 2]
        elif kind == "d3":
            (g,) = at
            total = s1[g, part(z, eighth)]
            for i in range(Z - 1):
                total += dr2[g, i]
            res[g, y, part(z, eighth)] = total
        elif kind == "d5":
            (g,) = at
            rows = slice(2 * g * BLOCK, 2 * (g + 1) * BLOCK)
            g_ref[rows] = d_ref[rows] - res[g].reshape(2 * BLOCK, BLOCK)

    copies = {}
    waited = set()
    for _, task in order:
        for ident in task["needs"]:
            if ident not in waited:
                waited.add(ident)
                copies[ident].wait_recv()
        body(task["name"])
        for ident, _, _ in task["sends"]:
            source, target, where = ends(ident)
            n = len(copies)
            copies[ident] = pltpu.make_async_remote_copy(
                src_ref=source, dst_ref=target, send_sem=send_sem.at[n], recv_sem=recv_sem.at[n],
                device_id=where, device_id_type=pl.DeviceIdType.MESH,
            )
            copies[ident].start()
    for ident, copy in copies.items():
        if ident not in waited:
            copy.wait_recv()
        copy.wait_send()


def local(top_inverse, panels, fill_pattern, diagonal_part):
    order, _ = make_plan().order()
    count = sum(len(task["sends"]) for _, task in order)
    f32, bf16 = jnp.float32, jnp.bfloat16
    depth = Z * ROWS
    scratch = [
        pltpu.VMEM((X, CORES, Y, ROWS, ROWS), f32),
        pltpu.VMEM((Y * ROWS, depth), bf16),
        pltpu.VMEM((Y * ROWS, depth), bf16),
        pltpu.VMEM((CHUNKS, Z, ROWS, BLOCK), f32),
        pltpu.VMEM((2, depth, 2 * BLOCK), bf16),
        pltpu.VMEM((2, depth, 2 * BLOCK), bf16),
        pltpu.VMEM((GROUPS, 2 * BLOCK, BLOCK), f32),
        pltpu.VMEM((GROUPS, Y - 1, 2 * BLOCK // Y, BLOCK), f32),
        pltpu.VMEM((GROUPS, 2 * BLOCK // Y, BLOCK), f32),
        pltpu.VMEM((GROUPS, Z - 1, 2 * BLOCK // Y // Z, BLOCK), f32),
        pltpu.VMEM((GROUPS, Y, 2 * BLOCK // Y, BLOCK), f32),
        pltpu.SemaphoreType.DMA((count,)),
        pltpu.SemaphoreType.DMA((count,)),
    ]
    for wave in WAVES:
        width = len(wave) * BLOCK
        scratch += [
            pltpu.VMEM((Y, ROWS, width), f32),
            pltpu.VMEM((2, ROWS // 2, width), f32),
            pltpu.VMEM((2, ROWS, width), f32),
        ]
    vmem = pl.BlockSpec(memory_space=pltpu.VMEM)
    return pl.pallas_call(
        functools.partial(kernel, order),
        out_shape=(jax.ShapeDtypeStruct(panels.shape, f32), jax.ShapeDtypeStruct(diagonal_part.shape, f32)),
        in_specs=[vmem, vmem, pl.BlockSpec(memory_space=pltpu.SMEM), vmem],
        out_specs=(vmem, vmem),
        scratch_shapes=scratch,
        compiler_params=pltpu.CompilerParams(
            collective_id=0, has_side_effects=True, vmem_limit_bytes=60 * 1024 * 1024
        ),
        cost_estimate=pl.CostEstimate(flops=2 * 8192**3 // 256, bytes_accessed=5 * 2**20, transcendentals=0),
        name="selected_inverse",
    )(top_inverse, panels, fill_pattern, diagonal_part)


def solution(mesh):
    in_specs = (P("row", "col"), P("row", "col"), P("col", None), P("col", None))
    out_specs = (P("row", "col"), P("col", None))
    return jax.shard_map(local, mesh=mesh, in_specs=in_specs, out_specs=out_specs, check_vma=False)
```

time: 500 us -> 160 us (0.32)
  waiting for transfers between devices: 446 us -> 0 us
  Pallas kernels: 0 us -> 156 us
  matrix products: 32.8 us -> 0 us
  between operations: 13.8 us -> 0.65 us
    all_gather x2 -> x0, waiting for transfers between devices: 302 us -> none  [the longest x1 249 us: local(): lax.all_gather(scaled_panel, 'row', axis=0, tiled=True)]
    pallas_call x0 -> x1, Pallas kernels: none -> 156 us  [local(): pl.pallas_call(functools.partial(kernel, order), out_shape=(jax.ShapeDtyp...]
    psum x1 -> x0, waiting for transfers between devices: 143 us -> none  [local(): summed = lax.psum(diag_terms, 'row')]
    dot_general x2 -> x0, matrix products: 32.8 us -> none  [the longest x1 30.9 us: local(): jnp.dot(block_row, lax.all_gather(scaled_panel, 'row', axis=0, tiled=True...]
  transfers between devices with their start and end apart: 3 -> 0, of which waited for: 3 -> 0; matrix products, arithmetic and copies ran while one was open for 1% -> 0% of each run, Pallas kernels for 0% -> 0%
where the time goes in v1:
time: 160 us; the launch traced here: 159 us
  Pallas kernels  156 us (98%)
  local copies, waits for them, and re-layouts  3.16 us (2%)
    pallas_call x1, Pallas kernels, local(): pl.pallas_call(functools.partial(kernel, order), out_shape=(jax.ShapeDtyp...  156 us

profile of v1, /device:TPU:2, one launch (start us, length us, event | category | flops | bytes accessed | tf_op | source)
XLA Modules:
  0.0 159.5 jit_solution(17031953180900078118)
XLA Ops:
  0.6 155.7 %selected_inverse.1 = (f32[256,1024]{1,0:T(8,128)}, f32[1024,128]{1,0:T(8,128)}) custom-call(f32[256,1024]{1,0:T(8,128)} %a_ref.1, f32[256,1024]{1,0:T(8,128)} %p_ref.1, s32[8,64]{1,0:T(8,128)} %fill_ref.1, f32[1024,128]{1,0:T(8,128)} %d_ref.1), custom_call_target="tpu_custom_call" | custom-call | flops 4294967296 | bytes 5242880 | tf_op jit(solution)/shard_map/selected_inverse/pallas_call | solution.py:349
  156.3 0.0 copy-start
  156.3 2.4 %copy.8 = f32[256,1024]{1,0:T(8,128)} copy(f32[256,1024]{1,0:T(8,128)} %get-tuple-element.4) | data formatting | bytes 2097152
  158.7 0.0 copy-done
  158.7 0.8 copy.9
Async XLA Ops:
  156.3 2.4 %copy-start = (f32[1024,128]{1,0:T(8,128)S(1)}, f32[1024,128]{1,0:T(8,128)}, u32[]{:S(2)}) copy-start(f32[1024,128]{1,0:T(8,128)} %get-tuple-element.5) | copy-start | bytes 1572868
